TPU v7x, 1024 devices: a whole 4x4x32 slice. The times are simulated.
1024 devices in a mesh: ctx: 64 (over y, z_hi, x, core), head: 16 (over z_lo).
Axes of the slice: x: 4, y: 4, z: 32 (z_hi: 2, z_lo: 16; z = z_hi * 16 + z_lo), core: 2. Of those that a mesh axis runs over, the one named last changes fastest.
Arguments:
- queries: bfloat16 [16384, 8192], P('ctx', 'head'), may hold values from -120 to 120
- key_rows: bfloat16 [16384, 512], P('ctx'), may hold values from -4 to 4
- value_rows: bfloat16 [16384, 512], P('ctx'), may hold values from -6 to 6
- lengths: int32 [64], replicated, may hold values from 1 to 1024, 16384 in all
- out_weight: bfloat16 [8192, 8192], P('head'), may hold values from -0.0625 to 0.0625
Outputs:
- layer_out: bfloat16 [16384, 8192], P(('ctx', 'head'))
Inputs may be any that keep to these rules, and one draw needn't show every extreme that they name: The lengths of the 64 documents sum to 16384; the longest is exactly 1024.
All inputs are finite; a program needn't handle non-finite values.
Results may differ from a plain program's by a relative error of at most 0.023.
Values may be sent and summed in bfloat16 or wider, within the bound.
A program may use at most 64 MiB of HBM per device.

v0:
```python
import math

import jax
import jax.numpy as jnp
from jax import lax
from jax.sharding import PartitionSpec as P

HD = 128
GROUP = 16
SPAN = 4


big_negative = -1e30


def shifted(shard, axis, by):
    length = lax.axis_size(axis)
    pairs = [(i, i + by) for i in range(length) if 0 <= i + by < length]
    return lax.ppermute(shard, axis, pairs)


def document_of(positions, doc_ends):
    return jnp.sum((positions[:, None] >= doc_ends[None, :]).astype(jnp.int32), axis=1)


def absorb_block(
    running, query_heads, key_piece, value_piece, offset, query_pos, query_docs, doc_ends
):
    row_count = key_piece.shape[0]
    key_pos = offset + jnp.arange(row_count, dtype=jnp.int32)
    same_doc = query_docs[:, None] == document_of(key_pos, doc_ends)[None, :]
    allowed = same_doc & (key_pos[None, :] <= query_pos[:, None]) & (key_pos[None, :] >= 0)
    scores = jnp.einsum(
        "qhd,kd->hqk", query_heads, key_piece, preferred_element_type=jnp.float32
    ) * (1.0 / math.sqrt(HD))
    top_old, total_old, summed_old = running
    top_new = jnp.maximum(top_old, jnp.max(jnp.where(allowed[None], scores, big_negative), axis=2))
    expo = jnp.where(allowed[None], jnp.exp(scores - top_new[:, :, None]), 0.0)
    factor = jnp.exp(top_old - top_new)
    total_new = total_old * factor + jnp.sum(expo, axis=2)
    added = jnp.einsum(
        "hqk,kd->qhd", expo.astype(jnp.bfloat16), value_piece, preferred_element_type=jnp.float32
    )
    summed_new = summed_old * factor.T[:, :, None] + added
    return (top_new, total_new, summed_new)


def absorb(running, query_heads, key_piece, value_piece, offset, query_pos, query_docs, doc_ends):
    return absorb_block(
        running, query_heads, key_piece, value_piece, offset, query_pos, query_docs, doc_ends
    )


def body(queries, key_rows, value_rows, lengths, out_weight):
    rows_here = queries.shape[0]
    heads_here = queries.shape[1] // HD
    ctx_index = lax.axis_index("ctx")
    head_index = lax.axis_index("head")
    kv_index = head_index * heads_here // GROUP
    own_keys = lax.dynamic_slice_in_dim(key_rows, kv_index * HD, HD, 1)
    own_values = lax.dynamic_slice_in_dim(value_rows, kv_index * HD, HD, 1)
    doc_ends = jnp.cumsum(lengths)
    first_row = ctx_index * rows_here
    query_pos = first_row + jnp.arange(rows_here, dtype=jnp.int32)
    query_docs = document_of(query_pos, doc_ends)
    query_heads = queries.reshape(rows_here, heads_here, HD)
    running = (
        jnp.full((heads_here, rows_here), big_negative, jnp.float32),
        jnp.zeros((heads_here, rows_here), jnp.float32),
        jnp.zeros((rows_here, heads_here, HD), jnp.float32),
    )

    def fold_piece(current, pieces, offset):
        return absorb(
            current, query_heads, pieces[0], pieces[1], offset, query_pos, query_docs, doc_ends
        )

    running = fold_piece(running, (own_keys, own_values), first_row)
    for distance in range(1, SPAN + 1):
        earlier = shifted((own_keys, own_values), "ctx", distance)
        running = fold_piece(running, earlier, first_row - distance * rows_here)
    attended = (
        (running[2] / running[1].T[:, :, None])
        .astype(jnp.bfloat16)
        .reshape(rows_here, heads_here * HD)
    )
    layer_out = lax.psum_scatter(
        jnp.dot(attended, out_weight, preferred_element_type=jnp.float32).astype(jnp.bfloat16),
        "head",
        scatter_dimension=0,
        tiled=True,
    )
    return layer_out


def solution(mesh):
    placed = (P("ctx", "head"), P("ctx", None), P("ctx", None), P(), P("head", None))
    return jax.shard_map(
        body, mesh=mesh, in_specs=placed, out_specs=P(("ctx", "head"), None), check_vma=False
    )
```

profile of v0, /device:TPU:16, one launch (start us, length us, event | category | flops | bytes accessed | tf_op | source)
XLA Modules:
  0.0 359.7 jit_solution(18328602903605705132)
XLA Ops:
  6.5 0.9 constant_dynamic-slice_fusion.1
  7.4 2.8 collective-permute-start.4
  10.3 3.4 collective-permute-start.2
  13.7 2.9 collective-permute-start
  16.6 30.4 %collective-permute-start.6 = (bf16[256,128]{1,0:T(8,128)(2,1)S(1)}, bf16[256,128]{1,0:T(8,128)(2,1)S(1)}, u32[]{:S(2)}, u32[]{:S(2)}) collective-permute-start(bf16[256,128]{1,0:T(8,128)(2,1)S(1)} %constant_dynamic-slice_fusion.1), channel_id=1, source_target_pairs={{0,64},{16,80},{32,96},{48,112},{64,128},{80,144},{96,160},{112,17... | collective-permute-start | bytes 196616 | tf_op jit(solution)/shard_map/ppermute | solution.py:19
  47.0 0.9 constant_dynamic-slice_fusion
  48.0 3.4 collective-permute-start.3
  51.5 0.7 copy.30
  52.6 0.7 and_and_fusion.4
  53.7 1.9 collective-permute-start.5
  55.6 0.3 select_reduce_fusion.1
  56.0 3.0 collective-permute-start.7
  59.0 0.3 select_reduce_fusion.2
  59.4 12.5 %collective-permute-start.1 = (bf16[256,128]{0,1:T(8,128)(2,1)S(1)}, bf16[256,128]{0,1:T(8,128)(2,1)S(1)}, u32[]{:S(2)}, u32[]{:S(2)}) collective-permute-start(bf16[256,128]{0,1:T(8,128)(2,1)S(1)} %copy.47), channel_id=1, source_target_pairs={{0,16},{16,32},{32,48},{48,64},{64,80},{80,96},{96,112},{112,128},... | collective-permute-start | bytes 196616 | tf_op jit(solution)/shard_map/ppermute | solution.py:19
  72.2 0.3 select_reduce_fusion
  73.7 0.3 fusion.6
  74.0 22.0 %collective-permute-done.3 = bf16[256,128]{0,1:T(8,128)(2,1)S(1)} collective-permute-done((bf16[256,128]{0,1:T(8,128)(2,1)S(1)}, bf16[256,128]{0,1:T(8,128)(2,1)S(1)}, u32[]{:S(2)}, u32[]{:S(2)}) %collective-permute-start.3) | collective-permute-done | bytes 65568 | tf_op jit(solution)/shard_map/ppermute | solution.py:19
  96.0 0.3 convolution_bitcast_fusion.2
  96.4 0.3 convolution_bitcast_fusion.1
  96.7 0.3 convolution_bitcast_fusion
  97.1 19.8 %collective-permute-done.1 = bf16[256,128]{0,1:T(8,128)(2,1)S(1)} collective-permute-done((bf16[256,128]{0,1:T(8,128)(2,1)S(1)}, bf16[256,128]{0,1:T(8,128)(2,1)S(1)}, u32[]{:S(2)}, u32[]{:S(2)}) %collective-permute-start.1) | collective-permute-done | bytes 65568 | tf_op jit(solution)/shard_map/ppermute | solution.py:19
  116.9 0.4 fusion.15
  117.3 4.4 %convolution_convert_fusion = bf16[256,8192]{1,0:T(8,128)(2,1)} fusion(bf16[256,512]{0,1:T(8,128)(2,1)S(1)} %bitcast.222, bf16[512,8192]{1,0:T(8,128)(2,1)S(1)} %bitcast.221), kind=kOutput, calls=%fused_computation | convolution fusion | flops 2149580800 | bytes 12845056 | tf_op jit(solution)/shard_map/dot_general | solution.py:88
  121.8 231.1 %reduce-scatter.2.cloned.1.call-done = bf16[16,8192]{1,0:T(8,128)(2,1)} async-done(((bf16[256,8192]{1,0:T(8,128)(2,1)}), bf16[16,8192]{1,0:T(8,128)(2,1)}) %reduce-scatter.2.cloned.1.call-update) | async-done | bytes 262160 | tf_op jit(solution)/shard_map/reduce_scatter | solution.py:87
  (34 shorter events, 2.3 us)
Async XLA Ops:
  6.5 46.8 %copy-start = (bf16[256,512]{1,0:T(8,128)(2,1)S(1)}, bf16[256,512]{1,0:T(8,128)(2,1)}, u32[]{:S(2)}) copy-start(bf16[256,512]{1,0:T(8,128)(2,1)} %param.5) | copy-start | bytes 786436
  6.5 346.3 %reduce-scatter.2.cloned.1.call-start = ((), (), s32[]{:S(2)}) async-start(), calls=%async_computation.1 | async-start | bytes 4456448 | tf_op jit(solution)/shard_map/reduce_scatter | solution.py:87
  7.4 46.3 %collective-permute-start.4 = (bf16[256,128]{1,0:T(8,128)(2,1)S(1)}, bf16[256,128]{1,0:T(8,128)(2,1)S(1)}, u32[]{:S(2)}, u32[]{:S(2)}) collective-permute-start(bf16[256,128]{1,0:T(8,128)(2,1)S(1)} %constant_dynamic-slice_fusion.1), channel_id=1, source_target_pairs={{0,48},{16,64},{32,80},{48,96},{64,112},{80,128},{96,144},{112,160... | collective-permute-start | bytes 196616 | tf_op jit(solution)/shard_map/ppermute | solution.py:19
  10.3 45.7 %collective-permute-start.2 = (bf16[256,128]{1,0:T(8,128)(2,1)S(1)}, bf16[256,128]{1,0:T(8,128)(2,1)S(1)}, u32[]{:S(2)}, u32[]{:S(2)}) collective-permute-start(bf16[256,128]{1,0:T(8,128)(2,1)S(1)} %constant_dynamic-slice_fusion.1), channel_id=1, source_target_pairs={{0,32},{16,48},{32,64},{48,80},{64,96},{80,112},{96,128},{112,144}... | collective-permute-start | bytes 196616 | tf_op jit(solution)/shard_map/ppermute | solution.py:19
  13.7 45.7 %collective-permute-start = (bf16[256,128]{1,0:T(8,128)(2,1)S(1)}, bf16[256,128]{1,0:T(8,128)(2,1)S(1)}, u32[]{:S(2)}, u32[]{:S(2)}) collective-permute-start(bf16[256,128]{1,0:T(8,128)(2,1)S(1)} %constant_dynamic-slice_fusion.1), channel_id=1, source_target_pairs={{0,16},{16,32},{32,48},{48,64},{64,80},{80,96},{96,112},{112,128},... | collective-permute-start | bytes 196616 | tf_op jit(solution)/shard_map/ppermute | solution.py:19
  16.6 55.6 %collective-permute-start.6 = (bf16[256,128]{1,0:T(8,128)(2,1)S(1)}, bf16[256,128]{1,0:T(8,128)(2,1)S(1)}, u32[]{:S(2)}, u32[]{:S(2)}) collective-permute-start(bf16[256,128]{1,0:T(8,128)(2,1)S(1)} %constant_dynamic-slice_fusion.1), channel_id=1, source_target_pairs={{0,64},{16,80},{32,96},{48,112},{64,128},{80,144},{96,160},{112,17... | collective-permute-start | bytes 196616 | tf_op jit(solution)/shard_map/ppermute | solution.py:19
  48.0 48.0 %collective-permute-start.3 = (bf16[256,128]{0,1:T(8,128)(2,1)S(1)}, bf16[256,128]{0,1:T(8,128)(2,1)S(1)}, u32[]{:S(2)}, u32[]{:S(2)}) collective-permute-start(bf16[256,128]{0,1:T(8,128)(2,1)S(1)} %copy.47), channel_id=1, source_target_pairs={{0,32},{16,48},{32,64},{48,80},{64,96},{80,112},{96,128},{112,144}... | collective-permute-start | bytes 196616 | tf_op jit(solution)/shard_map/ppermute | solution.py:19
  53.7 42.7 %collective-permute-start.5 = (bf16[256,128]{0,1:T(8,128)(2,1)S(1)}, bf16[256,128]{0,1:T(8,128)(2,1)S(1)}, u32[]{:S(2)}, u32[]{:S(2)}) collective-permute-start(bf16[256,128]{0,1:T(8,128)(2,1)S(1)} %copy.47), channel_id=1, source_target_pairs={{0,48},{16,64},{32,80},{48,96},{64,112},{80,128},{96,144},{112,160... | collective-permute-start | bytes 196616 | tf_op jit(solution)/shard_map/ppermute | solution.py:19
  56.0 40.8 %collective-permute-start.7 = (bf16[256,128]{0,1:T(8,128)(2,1)S(1)}, bf16[256,128]{0,1:T(8,128)(2,1)S(1)}, u32[]{:S(2)}, u32[]{:S(2)}) collective-permute-start(bf16[256,128]{0,1:T(8,128)(2,1)S(1)} %copy.47), channel_id=1, source_target_pairs={{0,64},{16,80},{32,96},{48,112},{64,128},{80,144},{96,160},{112,17... | collective-permute-start | bytes 196616 | tf_op jit(solution)/shard_map/ppermute | solution.py:19
  59.4 57.5 %collective-permute-start.1 = (bf16[256,128]{0,1:T(8,128)(2,1)S(1)}, bf16[256,128]{0,1:T(8,128)(2,1)S(1)}, u32[]{:S(2)}, u32[]{:S(2)}) collective-permute-start(bf16[256,128]{0,1:T(8,128)(2,1)S(1)} %copy.47), channel_id=1, source_target_pairs={{0,16},{16,32},{32,48},{48,64},{64,80},{80,96},{96,112},{112,128},... | collective-permute-start | bytes 196616 | tf_op jit(solution)/shard_map/ppermute | solution.py:19
  72.6 44.7 %slice-start = ((s8[8388608]{0:T(1024)(128)(4,1)}), s8[4194304]{0:T(1024)(128)(4,1)S(1)}, s32[]{:S(2)}) async-start(s8[8388608]{0:T(1024)(128)(4,1)} %bitcast.220), calls=%async_computation.2 | async-start | bytes 8388608
  74.0 43.3 %slice-start.1 = ((s8[8388608]{0:T(1024)(128)(4,1)}), s8[4194304]{0:T(1024)(128)(4,1)S(1)}, s32[]{:S(2)}) async-start(s8[8388608]{0:T(1024)(128)(4,1)} %bitcast.220), calls=%async_computation.3 | async-start | bytes 8388608
Sparse Core Ops, SparseCore 0:
  121.9 230.9 reduce-scatter.1
where the time goes:
time: 360 us
  waiting for transfers between devices  273 us (76%)
  starting transfers between devices  60.5 us (17%)
  between operations  13.7 us (4%)
  matrix products  7.81 us (2%)
    reduce_scatter x1, waiting for transfers between devices, body(): lax.psum_scatter(jnp.dot(attended, out_weight, preferred_element_type=jnp...  231 us
    ppermute x8, starting transfers between devices, shifted(): return lax.ppermute(shard, axis, pairs)  60.5 us
    ppermute x8, waiting for transfers between devices, shifted(): return lax.ppermute(shard, axis, pairs)  41.8 us
  transfers between devices with their start and end apart: 9, of which 3 were waited for; matrix products, arithmetic and copies ran while one was open for 2% of the time, Pallas kernels for 0%

commit v1 on v0

v1 whole, which is shorter than its diff:
```python
import functools
import math

import jax
import jax.numpy as jnp
from jax import lax
from jax.experimental import pallas as pl
from jax.experimental.pallas import tpu as pltpu
from jax.sharding import PartitionSpec as P

MESH = pl.DeviceIdType.MESH
HD = 128
SPAN = 4
QUAD = 4
RUN = 8
REACH = 10
PIECES = 2
TILE = 1024
SCALE = math.log2(math.e) / math.sqrt(HD)
F32 = jnp.float32
BF16 = jnp.bfloat16


def kernel(
    cfg, q_ref, k_ref, v_ref, len_ref, w_ref, o_ref,
    kbuf, vbuf, fk, fv, wbuf, bias, att, swp, cbuf, slots,
    own_sem, w_sem, st_send, st_recv, quad_send, quad_recv, x_send, x_recv,
    swp_send, swp_recv, z_send, z_recv,
):
    n_ctx, planes, reach = cfg
    shift = planes - 1 - reach
    rows, width = q_ref.shape
    heads = width // HD
    columns = w_ref.shape[1]
    tile = min(TILE, columns)
    part = columns // PIECES
    quarter = rows // QUAD
    docs = len_ref.shape[1]

    ctx = lax.axis_index("ctx")
    p = lax.axis_index("head")
    unit = lax.rem(ctx, RUN)
    run_base = ctx - unit
    half = lax.rem(ctx // RUN, 2)
    other = ctx + RUN * (1 - 2 * half)
    kv = p // QUAD
    quad_pos = lax.rem(p, QUAD)
    mirror = planes - 1 - p
    next_run = lax.rem(ctx + RUN, n_ctx)
    prev_run = lax.rem(ctx + n_ctx - RUN, n_ctx)
    right = (jnp.where(p == planes - 1, other, ctx), lax.rem(p + 1, planes))
    left = (jnp.where(p == 0, other, ctx), lax.rem(p + planes - 1, planes))

    def run_mate(by):
        return (run_base + lax.rem(unit + by, RUN), p)

    def quad_mate(by):
        return (ctx, kv * QUAD + lax.rem(quad_pos + by, QUAD))

    kv_cols = pl.ds(pl.multiple_of(kv * HD, HD), HD)
    w_copy = pltpu.make_async_copy(w_ref, wbuf, w_sem)
    w_copy.start()
    own_rows = pl.ds(SPAN * rows, rows)
    own_copies = [
        pltpu.make_async_copy(src.at[:, kv_cols], dst.at[own_rows], own_sem.at[i])
        for i, (src, dst) in enumerate(((k_ref, kbuf), (v_ref, vbuf)))
    ]
    for copy in own_copies:
        copy.start()
    swp[...] = jnp.zeros_like(swp)

    barrier = pltpu.get_barrier_semaphore()
    greeted = [run_mate(m) for m in range(1, RUN)]
    greeted += [quad_mate(m) for m in range(1, QUAD)]
    greeted += [right, left, (next_run, mirror), (prev_run, mirror), (other, p)]
    for device in greeted:
        pl.semaphore_signal(barrier, inc=1, device_id=device, device_id_type=MESH)
    pl.semaphore_wait(barrier, len(greeted))

    def remote(src, dst, send, recv, device):
        return pltpu.make_async_remote_copy(
            src_ref=src, dst_ref=dst, send_sem=send, recv_sem=recv,
            device_id=device, device_id_type=MESH,
        )

    def span_copy(distance, which, source):
        dst = (kbuf, vbuf)[which].at[pl.ds((SPAN - distance) * rows, rows)]
        return remote(
            source, dst, x_send.at[distance - 1, which], x_recv.at[distance - 1, which],
            run_mate(distance),
        )

    def own_source(which):
        return (k_ref, v_ref)[which].at[:, kv_cols]

    def far_source(which):
        return (fk, fv)[which]

    mirror_kv = mirror // QUAD
    mirror_rows = pl.ds(pl.multiple_of(lax.rem(mirror, QUAD) * quarter, quarter), quarter)
    mirror_cols = pl.ds(pl.multiple_of(mirror_kv * HD, HD), HD)
    my_rows = pl.ds(pl.multiple_of(quad_pos * quarter, quarter), quarter)

    def cross_copy(which):
        return remote(
            (k_ref, v_ref)[which].at[mirror_rows, mirror_cols],
            (fk, fv)[which].at[mirror_rows],
            st_send.at[which], st_recv.at[which], (next_run, mirror),
        )

    def cross_arrival(which):
        piece = (fk, fv)[which].at[my_rows]
        return remote(piece, piece, st_send.at[which], st_recv.at[which], (next_run, mirror))

    def quad_copy(by, which):
        piece = (fk, fv)[which].at[my_rows]
        return remote(
            piece, piece, quad_send.at[by - 1, which], quad_recv.at[by - 1, which], quad_mate(by)
        )

    def quad_arrival(by, which):
        origin = lax.rem(quad_pos + QUAD - by, QUAD)
        piece = (fk, fv)[which].at[pl.ds(pl.multiple_of(origin * quarter, quarter), quarter)]
        return remote(
            piece, piece, quad_send.at[by - 1, which], quad_recv.at[by - 1, which], quad_mate(by)
        )

    far_side = unit >= RUN - SPAN

    @pl.when(far_side)
    def _():
        for which in (0, 1):
            cross_copy(which).start()

    for distance in range(1, SPAN + 1):
        @pl.when(unit + distance < RUN)
        def _():
            for which in (0, 1):
                span_copy(distance, which, own_source(which)).start()

    @pl.when(far_side)
    def _():
        for which in (0, 1):
            cross_arrival(which).wait_recv()
            for by in range(1, QUAD):
                quad_copy(by, which).start()
        for which in (0, 1):
            for by in range(1, QUAD):
                quad_arrival(by, which).wait_recv()
        for distance in range(1, SPAN + 1):
            @pl.when(unit + distance >= RUN)
            def _():
                for which in (0, 1):
                    span_copy(distance, which, far_source(which)).start()

    lengths = len_ref[...].astype(F32)
    at_row = lax.broadcasted_iota(jnp.int32, (docs, docs), 0)
    at_col = lax.broadcasted_iota(jnp.int32, (docs, docs), 1)
    column = jnp.sum(jnp.where(at_row == at_col, lengths, 0.0), axis=1, keepdims=True)
    ends = jnp.sum(jnp.where(at_row <= at_col, column, 0.0), axis=0, keepdims=True)
    first = ctx * rows
    query_pos = (first + lax.broadcasted_iota(jnp.int32, (rows, 1), 0)).astype(F32)
    start = jnp.max(jnp.where(ends <= query_pos, ends, 0.0), axis=1, keepdims=True)
    span_rows = (SPAN + 1) * rows
    key_pos = first - SPAN * rows + lax.broadcasted_iota(jnp.int32, (1, span_rows), 1)
    key_pos = key_pos.astype(F32)
    bias[...] = jnp.where((key_pos >= start) & (key_pos <= query_pos), 0.0, -1e30)

    for copy in own_copies:
        copy.wait()
    for distance in range(1, SPAN + 1):
        for which in (0, 1):
            span_copy(distance, which, far_source(which)).wait_recv()

    def one_head(head, carry):
        cols = pl.ds(pl.multiple_of(head * HD, HD), HD)
        scores = lax.dot_general(
            q_ref[:, cols], kbuf[...], (((1,), (1,)), ((), ())), preferred_element_type=F32
        )
        scores = scores * SCALE + bias[...]
        top = jnp.max(scores, axis=1, keepdims=True)
        expo = jnp.exp2(scores - top)
        total = jnp.sum(expo, axis=1, keepdims=True)
        summed = jnp.dot(expo.astype(BF16), vbuf[...], preferred_element_type=F32)
        att[:, cols] = (summed / total).astype(BF16)
        return carry

    lax.fori_loop(0, heads, one_head, 0)

    low, high = p < shift, p > reach
    count = jnp.where(low, shift - p, jnp.where(high, p - reach, 0))
    base = jnp.where(low, p + 1 + reach, 0)
    strip = rows // planes

    def swap_copy(t):
        return remote(
            att.at[pl.ds(pl.multiple_of((base + t) * strip, strip), strip)],
            swp.at[pl.ds(t * strip, strip)],
            swp_send.at[t], swp_recv.at[t], (other, p),
        )

    for t in range(shift):
        @pl.when(t < count)
        def _():
            swap_copy(t).start()

    w_copy.wait()

    def project(i, carry):
        cols = pl.ds(pl.multiple_of(i * tile, tile), tile)
        cbuf[:, cols] = jnp.dot(
            att[...], wbuf[:, cols], preferred_element_type=F32
        ).astype(BF16)
        return carry

    lax.fori_loop(0, columns // tile, project, 0)

    def reach_right(at):
        return jnp.maximum(jnp.minimum(reach, planes - 1 - at), shift)

    def reach_left(at):
        return jnp.maximum(jnp.minimum(reach, at), shift)

    far = (reach_right(p), reach_left(p))
    before = (reach_right(left[1]), reach_left(right[1]))
    target = (right, left)

    def chain_copy(way, d, piece):
        cols = pl.ds(piece * part, part)
        return remote(
            slots.at[way, d, :, cols], slots.at[way, d - 1, :, cols],
            z_send.at[way, piece], z_recv.at[way, d - 1, piece], target[way],
        )

    def block_rows(d, way):
        block = lax.rem(p + d, planes) if way == 0 else lax.rem(p + planes - d, planes)
        return pl.ds(pl.multiple_of(block * strip, strip), strip)

    def chain_step(s, carry):
        d = reach - s
        for piece in range(PIECES):
            cols = pl.ds(piece * part, part)
            for way in (0, 1):
                @pl.when(d <= far[way])
                def _():
                    own = block_rows(d, way)

                    @pl.when(d < before[way])
                    def _():
                        chain_copy(way, d + 1, piece).wait_recv()
                        slots[way, d, :, cols] = (
                            slots[way, d, :, cols].astype(F32) + cbuf[own, cols].astype(F32)
                        ).astype(BF16)

                    @pl.when(d >= before[way])
                    def _():
                        slots[way, d, :, cols] = cbuf[own, cols]

                    @pl.when(d < far[way])
                    def _():
                        chain_copy(way, d + 1, piece).wait_send()

                    chain_copy(way, d, piece).start()
        return carry

    lax.fori_loop(0, reach - shift, chain_step, 0)

    @pl.when(count > 0)
    def _():
        for t in range(shift):
            @pl.when(t < count)
            def _():
                swap_copy(t).wait_send()
                swap_copy(t).wait_recv()

        def project_swapped(i, carry):
            cols = pl.ds(pl.multiple_of(i * tile, tile), tile)
            product = jnp.dot(
                swp[...], wbuf[:, cols], preferred_element_type=F32
            ).astype(BF16)
            for t in range(shift):
                @pl.when(t < count)
                def _():
                    into = pl.ds(pl.multiple_of((base + t) * strip, strip), strip)
                    cbuf[into, cols] = product[t * strip:(t + 1) * strip]
            return carry

        lax.fori_loop(0, columns // tile, project_swapped, 0)

    lax.fori_loop(reach - shift, reach, chain_step, 0)

    mine = pl.ds(pl.multiple_of(p * strip, strip), strip)
    for piece in range(PIECES):
        cols = pl.ds(piece * part, part)
        for way in (0, 1):
            chain_copy(way, 1, piece).wait_recv()
        o_ref[:, cols] = (
            slots[0, 0, :, cols].astype(F32)
            + slots[1, 0, :, cols].astype(F32)
            + cbuf[mine, cols].astype(F32)
        ).astype(BF16)

    for piece in range(PIECES):
        for way in (0, 1):
            chain_copy(way, 1, piece).wait_send()
    for distance in range(1, SPAN + 1):
        for which in (0, 1):
            span_copy(distance, which, far_source(which)).wait_send()

    @pl.when(far_side)
    def _():
        for which in (0, 1):
            cross_copy(which).wait_send()
            for by in range(1, QUAD):
                quad_copy(by, which).wait_send()


def solution(mesh, reach=REACH):
    n_ctx, planes = mesh.shape["ctx"], mesh.shape["head"]
    shift = planes - 1 - reach

    def body(queries, key_rows, value_rows, lengths, out_weight):
        rows, width = queries.shape
        columns = out_weight.shape[1]
        strip = rows // planes
        span_rows = (SPAN + 1) * rows
        vmem = pl.BlockSpec(memory_space=pltpu.VMEM)
        hbm = pl.BlockSpec(memory_space=pl.ANY)
        dma = pltpu.SemaphoreType.DMA
        return pl.pallas_call(
            functools.partial(kernel, (n_ctx, planes, reach)),
            out_shape=jax.ShapeDtypeStruct((strip, columns), BF16),
            in_specs=[vmem, hbm, hbm, vmem, hbm],
            out_specs=vmem,
            scratch_shapes=[
                pltpu.VMEM((span_rows, HD), BF16),
                pltpu.VMEM((span_rows, HD), BF16),
                pltpu.VMEM((rows, HD), BF16),
                pltpu.VMEM((rows, HD), BF16),
                pltpu.VMEM(out_weight.shape, BF16),
                pltpu.VMEM((rows, span_rows), F32),
                pltpu.VMEM((rows, width), BF16),
                pltpu.VMEM((shift * strip, width), BF16),
                pltpu.VMEM((rows, columns), BF16),
                pltpu.VMEM((2, reach + 1, strip, columns), BF16),
                dma((2,)),
                dma,
                dma((2,)),
                dma((2,)),
                dma((QUAD - 1, 2)),
                dma((QUAD - 1, 2)),
                dma((SPAN, 2)),
                dma((SPAN, 2)),
                dma((shift,)),
                dma((shift,)),
                dma((2, PIECES)),
                dma((2, reach, PIECES)),
            ],
            compiler_params=pltpu.CompilerParams(
                collective_id=0, has_side_effects=True, vmem_limit_bytes=48 * 1024 * 1024
            ),
        )(queries, key_rows, value_rows, lengths.reshape(1, -1), out_weight)

    placed = (P("ctx", "head"), P("ctx", None), P("ctx", None), P(), P("head", None))
    return jax.shard_map(
        body, mesh=mesh, in_specs=placed, out_specs=P(("ctx", "head"), None), check_vma=False
    )
```

time: 360 us -> 121 us (0.34)
  waiting for transfers between devices: 273 us -> 0 us
  Pallas kernels: 0 us -> 117 us
  starting transfers between devices: 60.5 us -> 0 us
  between operations: 13.7 us -> 0.01 us
  matrix products: 7.81 us -> 0 us
    reduce_scatter x1 -> x0, waiting for transfers between devices: 231 us -> none  [body(): lax.psum_scatter(jnp.dot(attended, out_weight, preferred_element_type=jnp...]
    pallas_call x0 -> x1, Pallas kernels: none -> 117 us  [body(): pl.pallas_call(functools.partial(kernel, (n_ctx, planes, reach)), out_sha...]
    ppermute x8 -> x0, starting transfers between devices: 60.5 us -> none  [shifted(): return lax.ppermute(shard, axis, pairs)]
    ppermute x8 -> x0, waiting for transfers between devices: 41.8 us -> none  [shifted(): return lax.ppermute(shard, axis, pairs)]
    dot_general x11 -> x0, matrix products: 7.81 us -> none  [the longest x1 4.44 us: body(): jnp.dot(attended, out_weight, preferred_element_type=jnp.float32)]
    unnamed x7 -> x9, local copies, waits for them, and re-layouts: 0.13 us -> 4.21 us
  transfers between devices with their start and end apart: 9 -> 0, of which waited for: 3 -> 0; matrix products, arithmetic and copies ran while one was open for 2% -> 0% of each run, Pallas kernels for 0% -> 0%
where the time goes in v1:
time: 121 us
  Pallas kernels  117 us (97%)
  local copies, waits for them, and re-layouts  4.21 us (3%)
    pallas_call x1, Pallas kernels, body(): pl.pallas_call(functools.partial(kernel, (n_ctx, planes, reach)), out_sha...  117 us
    unnamed x9, local copies, waits for them, and re-layouts  4.21 us

profile of v1, /device:TPU:16, one launch (start us, length us, event | category | flops | bytes accessed | tf_op | source)
XLA Modules:
  0.0 120.9 jit_solution(1124434848804306003)
XLA Ops:
  0.0 0.0 copy-start
  0.0 0.9 copy-done
  1.0 0.0 copy-start.1
  1.0 0.9 copy-done.1
  1.9 0.0 copy-start.2
  1.9 0.9 copy-done.2
  2.9 0.0 copy-start.3
  2.9 0.7 copy-done.3
  3.5 116.7 %shard_map.55 = bf16[16,8192]{1,0:T(8,128)(2,1)S(1)} custom-call(bf16[256,512]{1,0:T(8,128)(2,1)S(1)} %copy-done, bf16[256,512]{1,0:T(8,128)(2,1)S(1)} %copy-done.1, bf16[256,512]{1,0:T(8,128)(2,1)S(1)} %copy-done.2, s32[1,64]{1,0:T(1,128)S(1)} %bitcast.1, bf16[512,8192]{1,0:T(8,128)(2,1)} %w_ref.1), custom_call_target="tpu_custom_call" | custom-call | tf_op jit(solution)/shard_map/pallas_call | solution.py:330
  120.2 0.7 copy.7
Async XLA Ops:
  0.0 0.9 copy-start
  1.0 0.9 copy-start.1
  1.9 0.9 copy-start.2
  2.9 0.7 copy-start.3
